TPU v7x, 32 devices: a whole 2x2x4 slice. The times are simulated.
32 devices in a mesh: groups: 2 (over x), view: 16 (over z, y, core).
Axes of the slice: x: 2, y: 2, z: 4, core: 2. Of those that a mesh axis runs over, the one named last changes fastest.
Arguments:
- query: bfloat16 [4096, 1024], P(('groups', 'view')), parts along dimension 0, may hold values from -28 to 28
- keys: bfloat16 [4096, 1024], P(('groups', 'view')), parts along dimension 0, may hold values from -6 to 6
- values: bfloat16 [4096, 1024], P(('groups', 'view')), parts along dimension 0, may hold values from -6 to 6
- grad_out: bfloat16 [4096, 1024], P(('groups', 'view')), parts along dimension 0, may hold values from -6 to 6
- margin: int32 [32, 4, 1, 1], P('groups'), parts along dimension 0, may hold values 0 or 1
Outputs:
- attended: bfloat16 [4096, 1024], P(('groups', 'view')), parts along dimension 0
- grad_query: bfloat16 [4096, 1024], P(('groups', 'view')), parts along dimension 0
- grad_key: bfloat16 [4096, 1024], P(('groups', 'view')), parts along dimension 0
- grad_value: bfloat16 [4096, 1024], P(('groups', 'view')), parts along dimension 0
There are 2 independent parts, one for each index of `groups`. A program takes and returns all parts, laid end to end along the dimension named above; each array names one. Nothing has to cross between parts.
All inputs are finite; a program needn't handle non-finite values.
Results may differ from a plain program's by a relative error of at most 0.033.
Values may be sent and summed in bfloat16 or wider, within the bound.
A program may use at most 64 MiB of HBM per device.

v0:
```python
import math

import jax
import jax.numpy as jnp
from jax import lax
from jax.sharding import PartitionSpec as P

H = 8
BLK = 128
SPAN = 2


NEG_FILL = -1e30


def from_behind(block, axis, distance):
    devices = range(lax.axis_size(axis))
    route = [((i - distance) % len(devices), i) for i in devices]
    return lax.ppermute(block, axis, route)


def mask_spans_of(margin, image_index, reach):
    mask_row = lax.dynamic_index_in_dim(margin, image_index, 0, keepdims=False)
    filled = jnp.ones((1,) + mask_row.shape[1:], mask_row.dtype)
    return jnp.concatenate([mask_row[:reach], filled, mask_row[reach:]], axis=0)


def block_allowed(mask_spans, block_rows):
    span_count, block_count, _ = mask_spans.shape
    block_grid = jnp.transpose(mask_spans, (1, 0, 2)).reshape(block_count, span_count * block_count)
    return jnp.repeat(jnp.repeat(block_grid, block_rows, axis=0), block_rows, axis=1) > 0


def body(query, keys, values, grad_out, margin):
    tokens = query.shape[0]
    row_width = query.shape[1]
    head_dim = row_width // H
    score_scale = 1.0 / math.sqrt(head_dim)
    position = lax.axis_index("view")
    key_value = jnp.stack((keys, values))
    arrived = {0: key_value}
    forward_piece = key_value
    for hop_index in range(1, SPAN + 1):
        forward_piece = from_behind(forward_piece, "view", -1)
        arrived[hop_index] = forward_piece
    backward_piece = key_value
    for hop_index in range(1, SPAN + 1):
        backward_piece = from_behind(backward_piece, "view", 1)
        arrived[-hop_index] = backward_piece
    stacked = jnp.concatenate([arrived[offset] for offset in range(-SPAN, SPAN + 1)], axis=1)
    key_all = stacked[0].reshape(-1, H, head_dim)
    value_all = stacked[1].reshape(-1, H, head_dim)
    query_heads = query.reshape(tokens, H, head_dim)
    grad_heads = grad_out.reshape(tokens, H, head_dim)
    mask_full = mask_spans_of(margin, position, SPAN)
    allowed = block_allowed(mask_full, BLK)
    scores = (
        jnp.einsum("qhd,khd->hqk", query_heads, key_all, preferred_element_type=jnp.float32)
        * score_scale
    )
    scores = jnp.where(allowed[None], scores, NEG_FILL)
    row_max = jnp.max(scores, axis=-1, keepdims=True)
    log_total = row_max + jnp.log(jnp.sum(jnp.exp(scores - row_max), axis=-1, keepdims=True))
    prob_full = jnp.exp(scores - log_total)
    prob_half = prob_full.astype(jnp.bfloat16)
    attended = jnp.einsum(
        "hqk,khd->qhd", prob_half, value_all, preferred_element_type=jnp.float32
    ).astype(jnp.bfloat16)
    row_dot = jnp.sum(grad_heads.astype(jnp.float32) * attended.astype(jnp.float32), axis=-1)
    row_dot = jnp.transpose(row_dot)[..., None]
    prob_grad = jnp.einsum(
        "qhd,khd->hqk", grad_heads, value_all, preferred_element_type=jnp.float32
    )
    grad_half = (prob_full * (prob_grad - row_dot)).astype(jnp.bfloat16)
    grad_query = (
        jnp.einsum("hqk,khd->qhd", grad_half, key_all, preferred_element_type=jnp.float32)
        * score_scale
    )
    grad_query = grad_query.astype(jnp.bfloat16).reshape(tokens, row_width)

    def pair_terms(pair_index):
        start = pair_index * tokens
        grad_cols = grad_half[:, :, start : start + tokens]
        prob_cols = prob_half[:, :, start : start + tokens]
        key_part = jnp.einsum(
            "hqk,qhd->khd", grad_cols, query_heads, preferred_element_type=jnp.float32
        )
        value_part = jnp.einsum(
            "hqk,qhd->khd", prob_cols, grad_heads, preferred_element_type=jnp.float32
        )
        return jnp.stack((key_part, value_part)).reshape(2, tokens, row_width)

    terms = {}
    for offset in range(-SPAN, SPAN + 1):
        if offset == 0:
            terms[offset] = pair_terms(SPAN)
        else:
            terms[offset] = pair_terms(offset + SPAN)
    upward = terms[SPAN]
    for hop_index in range(1, SPAN + 1):
        upward = from_behind(upward, "view", 1)
        if hop_index < SPAN:
            upward = upward + terms[SPAN - hop_index]
    downward = terms[-SPAN]
    for hop_index in range(1, SPAN + 1):
        downward = from_behind(downward, "view", -1)
        if hop_index < SPAN:
            downward = downward + terms[hop_index - SPAN]
    totals = terms[0] + upward + downward
    grad_key = (totals[0] * score_scale).astype(jnp.bfloat16)
    grad_value = totals[1].astype(jnp.bfloat16)
    return (attended.reshape(tokens, row_width), grad_query, grad_key, grad_value)


def solution(mesh):
    return jax.shard_map(
        body,
        mesh=mesh,
        in_specs=(
            P(("groups", "view"), None),
            P(("groups", "view"), None),
            P(("groups", "view"), None),
            P(("groups", "view"), None),
            P("groups", None, None, None),
        ),
        out_specs=(
            P(("groups", "view"), None),
            P(("groups", "view"), None),
            P(("groups", "view"), None),
            P(("groups", "view"), None),
        ),
        check_vma=False,
    )
```

profile of v0, /device:TPU:1, one launch (start us, length us, event | category | flops | bytes accessed | tf_op | source)
XLA Modules:
  0.0 107.7 jit_solution(15547164735799285519)
XLA Ops:
  0.7 1.2 %copy.44 = bf16[128,1024]{0,1:T(8,128)(2,1)S(1)} copy(bf16[128,1024]{1,0:T(8,128)(2,1)} %param.6) | data formatting | bytes 524288 | tf_op args[1]
  1.8 1.1 %copy.45 = bf16[128,1024]{0,1:T(8,128)(2,1)S(1)} copy(bf16[128,1024]{1,0:T(8,128)(2,1)} %param.7) | data formatting | bytes 524288 | tf_op args[2]
  3.0 2.7 %collective-permute-start = (bf16[2,128,1024]{1,2,0:T(8,128)(2,1)S(1)}, bf16[2,128,1024]{1,2,0:T(8,128)(2,1)S(1)}, u32[]{:S(2)}, u32[]{:S(2)}) collective-permute-start(bf16[2,128,1024]{1,2,0:T(8,128)(2,1)S(1)} %pad_maximum_fusion.2), channel_id=1, source_target_pairs={{15,0},{0,1},{1,2},{2,3},{3,4},{4,5},{5,6},{6,7},{7,8},{8,9},{9,10... | collective-permute-start | bytes 1572872 | tf_op jit(solution)/shard_map/ppermute | solution.py:19
  5.7 11.7 %collective-permute-done = bf16[2,128,1024]{1,2,0:T(8,128)(2,1)S(1)} collective-permute-done((bf16[2,128,1024]{1,2,0:T(8,128)(2,1)S(1)}, bf16[2,128,1024]{1,2,0:T(8,128)(2,1)S(1)}, u32[]{:S(2)}, u32[]{:S(2)}) %collective-permute-start) | collective-permute-done | bytes 524320 | tf_op jit(solution)/shard_map/ppermute | solution.py:19
  17.4 2.5 %collective-permute-start.1 = (bf16[2,128,1024]{1,2,0:T(8,128)(2,1)S(1)}, bf16[2,128,1024]{1,2,0:T(8,128)(2,1)S(1)}, u32[]{:S(2)}, u32[]{:S(2)}) collective-permute-start(bf16[2,128,1024]{1,2,0:T(8,128)(2,1)S(1)} %collective-permute-done), channel_id=1, source_target_pairs={{15,0},{0,1},{1,2},{2,3},{3,4},{4,5},{5,6},{6,7},{7,8},{8,9},{9,10... | collective-permute-start | bytes 1572872 | tf_op jit(solution)/shard_map/ppermute | solution.py:19
  20.5 1.1 %copy.95 = bf16[128,1024]{0,1:T(8,128)(2,1)S(1)} copy(bf16[128,1024]{1,0:T(8,128)(2,1)} %param.5) | data formatting | bytes 524288 | tf_op jit(solution)/shard_map/reshape | solution.py:53
  21.6 9.6 %collective-permute-done.1 = bf16[2,128,1024]{1,2,0:T(8,128)(2,1)S(1)} collective-permute-done((bf16[2,128,1024]{1,2,0:T(8,128)(2,1)S(1)}, bf16[2,128,1024]{1,2,0:T(8,128)(2,1)S(1)}, u32[]{:S(2)}, u32[]{:S(2)}) %collective-permute-start.1) | collective-permute-done | bytes 524320 | tf_op jit(solution)/shard_map/ppermute | solution.py:19
  35.1 1.2 %fusion.16 = f32[8,128,128]{1,2,0:T(8,128)} fusion(bf16[128,8,128]{0,2,1:T(8,128)(2,1)S(1)} %bitcast.98, bf16[8,128,640]{1,2,0:T(8,128)(2,1)S(1)} %fusion), kind=kOutput, calls=%fused_computation.32 | convolution fusion | flops 33554432 | bytes 1048576 | tf_op jit(solution)/shard_map/hqk,qhd->khd/dot_general | solution.py:85
  36.3 1.1 %fusion.24 = f32[8,128,128]{1,2,0:T(8,128)} fusion(bf16[128,8,128]{0,2,1:T(8,128)(2,1)S(1)} %bitcast.99, bf16[8,128,640]{1,2,0:T(8,128)(2,1)S(1)} %fusion), kind=kOutput, calls=%fused_computation.40 | convolution fusion | flops 33554432 | bytes 1048576 | tf_op jit(solution)/shard_map/hqk,qhd->khd/dot_general | solution.py:85
  39.7 2.0 %copy.71 = f32[1,128,1024]{2,1,0:T(8,128)} copy(f32[1,128,1024]{1,2,0:T(8,128)} %bitcast.114) | data formatting | bytes 1048576 | tf_op jit(solution)/shard_map/stack | solution.py:91
  41.7 2.0 %copy.61 = f32[1,128,1024]{2,1,0:T(8,128)} copy(f32[1,128,1024]{1,2,0:T(8,128)} %bitcast.113) | data formatting | bytes 1048576 | tf_op jit(solution)/shard_map/stack | solution.py:91
  43.7 2.1 %copy.72 = f32[1,128,1024]{2,1,0:T(8,128)} copy(f32[1,128,1024]{1,2,0:T(8,128)} %bitcast.112) | data formatting | bytes 1048576 | tf_op jit(solution)/shard_map/stack | solution.py:91
  45.8 2.0 %copy.62 = f32[1,128,1024]{2,1,0:T(8,128)} copy(f32[1,128,1024]{1,2,0:T(8,128)} %bitcast.111) | data formatting | bytes 1048576 | tf_op jit(solution)/shard_map/stack | solution.py:91
  47.8 2.4 %pad_maximum_fusion = f32[2,128,1024]{2,1,0:T(8,128)} fusion(f32[1,128,1024]{2,1,0:T(8,128)} %copy.62, f32[1,128,1024]{2,1,0:T(8,128)} %copy.61), kind=kLoop, calls=%fused_computation.15 | loop fusion | flops 262144 | bytes 2097152 | tf_op jit(solution)/shard_map/stack | solution.py:91
  50.2 2.4 %collective-permute-start.4 = (f32[2,128,1024]{2,1,0:T(8,128)}, f32[2,128,1024]{2,1,0:T(8,128)}, u32[]{:S(2)}, u32[]{:S(2)}) collective-permute-start(f32[2,128,1024]{2,1,0:T(8,128)} %pad_maximum_fusion), channel_id=1, source_target_pairs={{15,0},{0,1},{1,2},{2,3},{3,4},{4,5},{5,6},{6,7},{7,8},{8,9},{9,10... | collective-permute-start | bytes 3145736 | tf_op jit(solution)/shard_map/ppermute | solution.py:19
  53.8 2.1 %fusion.12 = f32[8,128,128]{1,2,0:T(8,128)} fusion(bf16[128,8,128]{0,2,1:T(8,128)(2,1)S(1)} %bitcast.100, bf16[8,128,640]{1,2,0:T(8,128)(2,1)} %copy-done), kind=kOutput, calls=%fused_computation.28 | convolution fusion | flops 33554432 | bytes 1048576 | tf_op jit(solution)/shard_map/hqk,qhd->khd/dot_general | solution.py:85
  55.8 2.1 %copy.76 = f32[1,128,1024]{2,1,0:T(8,128)} copy(f32[1,128,1024]{1,2,0:T(8,128)} %bitcast.117) | data formatting | bytes 1048576 | tf_op jit(solution)/shard_map/stack | solution.py:91
  57.9 2.1 %fusion.20 = f32[8,128,128]{1,2,0:T(8,128)} fusion(bf16[128,8,128]{0,2,1:T(8,128)(2,1)S(1)} %bitcast.101, bf16[8,128,640]{1,2,0:T(8,128)(2,1)} %copy-done), kind=kOutput, calls=%fused_computation.36 | convolution fusion | flops 33554432 | bytes 1048576 | tf_op jit(solution)/shard_map/hqk,qhd->khd/dot_general | solution.py:85
  59.9 2.0 %copy.66 = f32[1,128,1024]{2,1,0:T(8,128)} copy(f32[1,128,1024]{1,2,0:T(8,128)} %bitcast.118) | data formatting | bytes 1048576 | tf_op jit(solution)/shard_map/stack | solution.py:91
  62.0 1.1 %fusion.10 = f32[8,128,128]{1,2,0:T(8,128)} fusion(bf16[128,8,128]{0,2,1:T(8,128)(2,1)S(1)} %bitcast.94, bf16[8,128,640]{1,2,0:T(8,128)(2,1)S(1)} %fusion.4), kind=kOutput, calls=%fused_computation.26 | convolution fusion | flops 33554432 | bytes 1048576 | tf_op jit(solution)/shard_map/hqk,qhd->khd/dot_general | solution.py:88
  63.1 2.1 %copy.77 = f32[1,128,1024]{2,1,0:T(8,128)} copy(f32[1,128,1024]{1,2,0:T(8,128)} %bitcast.119) | data formatting | bytes 1048576 | tf_op jit(solution)/shard_map/stack | solution.py:91
  65.1 1.1 %fusion.18 = f32[8,128,128]{1,2,0:T(8,128)} fusion(bf16[128,8,128]{0,2,1:T(8,128)(2,1)S(1)} %bitcast.95, bf16[8,128,640]{1,2,0:T(8,128)(2,1)S(1)} %fusion.4), kind=kOutput, calls=%fused_computation.34 | convolution fusion | flops 33554432 | bytes 1048576 | tf_op jit(solution)/shard_map/hqk,qhd->khd/dot_general | solution.py:88
  66.2 2.0 %copy.67 = f32[1,128,1024]{2,1,0:T(8,128)} copy(f32[1,128,1024]{1,2,0:T(8,128)} %bitcast.120) | data formatting | bytes 1048576 | tf_op jit(solution)/shard_map/stack | solution.py:91
  68.3 7.7 %collective-permute-done.4 = f32[2,128,1024]{2,1,0:T(8,128)} collective-permute-done((f32[2,128,1024]{2,1,0:T(8,128)}, f32[2,128,1024]{2,1,0:T(8,128)}, u32[]{:S(2)}, u32[]{:S(2)}) %collective-permute-start.4) | collective-permute-done | bytes 1048608 | tf_op jit(solution)/shard_map/ppermute | solution.py:19
  76.0 2.7 %maximum_add_fusion.1 = f32[2,128,1024]{2,1,0:T(8,128)} fusion(f32[2,128,1024]{2,1,0:T(8,128)} %collective-permute-done.4, f32[1,128,1024]{2,1,0:T(8,128)} %copy.67, f32[1,128,1024]{2,1,0:T(8,128)} %copy.66), kind=kLoop, calls=%fused_computation.16 | loop fusion | flops 524288 | bytes 3145728 | tf_op jit(solution)/shard_map/add | solution.py:103
  78.6 2.5 %collective-permute-start.5 = (f32[2,128,1024]{2,1,0:T(8,128)}, f32[2,128,1024]{2,1,0:T(8,128)}, u32[]{:S(2)}, u32[]{:S(2)}) collective-permute-start(f32[2,128,1024]{2,1,0:T(8,128)} %maximum_add_fusion.1), channel_id=1, source_target_pairs={{15,0},{0,1},{1,2},{2,3},{3,4},{4,5},{5,6},{6,7},{7,8},{8,9},{9,10... | collective-permute-start | bytes 3145736 | tf_op jit(solution)/shard_map/ppermute | solution.py:19
  81.1 2.3 %maximum_add_fusion.2 = f32[2,128,1024]{2,1,0:T(8,128)} fusion(f32[2,128,1024]{2,1,0:T(8,128)} %collective-permute-done.6, f32[1,128,1024]{2,1,0:T(8,128)S(1)} %copy-done.3, f32[1,128,1024]{2,1,0:T(8,128)S(1)} %copy-done.2), kind=kLoop, calls=%fused_computation.18 | loop fusion | flops 524288 | bytes 3145728 | tf_op jit(solution)/shard_map/add | solution.py:108
  83.5 1.2 %fusion.5 = bf16[8,128,128]{2,1,0:T(8,128)(2,1)} fusion(bf16[640,8,128]{0,2,1:T(8,128)(2,1)S(1)} %bitcast.104, bf16[8,128,640]{1,2,0:T(8,128)(2,1)S(1)} %copy-done.1), kind=kOutput, calls=%fused_computation.12 | convolution fusion | flops 168034304 | bytes 2883584 | tf_op jit(solution)/shard_map/hqk,khd->qhd/dot_general | solution.py:76
  84.7 1.8 %copy.79 = bf16[128,1024]{1,0:T(8,128)(2,1)} copy(bf16[128,1024]{0,1:T(8,128)(2,1)} %bitcast.122) | data formatting | bytes 524288
  87.3 1.3 %fusion.28 = f32[8,128,128]{1,2,0:T(8,128)S(1)} fusion(bf16[128,8,128]{0,2,1:T(8,128)(2,1)S(1)} %bitcast.102, bf16[8,128,640]{1,2,0:T(8,128)(2,1)} %copy-done), kind=kOutput, calls=%fused_computation.44 | convolution fusion | flops 33554432 | bytes 1048576 | tf_op jit(solution)/shard_map/hqk,qhd->khd/dot_general | solution.py:85
  89.3 15.1 %collective-permute-done.5 = f32[2,128,1024]{2,1,0:T(8,128)} collective-permute-done((f32[2,128,1024]{2,1,0:T(8,128)}, f32[2,128,1024]{2,1,0:T(8,128)}, u32[]{:S(2)}, u32[]{:S(2)}) %collective-permute-start.5) | collective-permute-done | bytes 1048608 | tf_op jit(solution)/shard_map/ppermute | solution.py:19
  104.4 1.8 %fusion.6 = f32[2,128,1024]{2,1,0:T(8,128)S(1)} fusion(f32[2,128,1024]{2,1,0:T(8,128)} %collective-permute-done.7, f32[2,128,1024]{2,1,0:T(8,128)} %collective-permute-done.5, f32[1,128,1024]{2,1,0:T(8,128)S(1)} %copy.57, f32[1,128,1024]{2,1,0:T(8,128)S(1)} %copy.56), kind=kLoop, calls=%fused_computation.14 | loop fusion | flops 786432 | bytes 4194304 | tf_op jit(solution)/shard_map/add | solution.py:109
  (50 shorter events, 10.8 us)
Async XLA Ops:
  0.6 19.3 %copy-start.7 = (s32[16,4,1,1]{0,3,2,1:T(1,128)S(1)}, s32[16,4,1,1]{0,3,2,1:T(1,128)}, u32[]{:S(2)}) copy-start(s32[16,4,1,1]{0,3,2,1:T(1,128)} %param.9) | copy-start | bytes 772
  0.6 19.7 %copy-start.6 = (bf16[128,1024]{1,0:T(8,128)(2,1)S(1)}, bf16[128,1024]{1,0:T(8,128)(2,1)}, u32[]{:S(2)}) copy-start(bf16[128,1024]{1,0:T(8,128)(2,1)} %param.8) | copy-start | bytes 786436
  3.0 14.4 %collective-permute-start = (bf16[2,128,1024]{1,2,0:T(8,128)(2,1)S(1)}, bf16[2,128,1024]{1,2,0:T(8,128)(2,1)S(1)}, u32[]{:S(2)}, u32[]{:S(2)}) collective-permute-start(bf16[2,128,1024]{1,2,0:T(8,128)(2,1)S(1)} %pad_maximum_fusion.2), channel_id=1, source_target_pairs={{15,0},{0,1},{1,2},{2,3},{3,4},{4,5},{5,6},{6,7},{7,8},{8,9},{9,10... | collective-permute-start | bytes 1572872 | tf_op jit(solution)/shard_map/ppermute | solution.py:19
  5.7 14.5 %collective-permute-start.2 = (bf16[2,128,1024]{1,2,0:T(8,128)(2,1)S(1)}, bf16[2,128,1024]{1,2,0:T(8,128)(2,1)S(1)}, u32[]{:S(2)}, u32[]{:S(2)}) collective-permute-start(bf16[2,128,1024]{1,2,0:T(8,128)(2,1)S(1)} %pad_maximum_fusion.2), channel_id=1, source_target_pairs={{1,0},{2,1},{3,2},{4,3},{5,4},{6,5},{7,6},{8,7},{9,8},{10,9},{11,1... | collective-permute-start | bytes 1572872 | tf_op jit(solution)/shard_map/ppermute | solution.py:19
  17.4 13.8 %collective-permute-start.1 = (bf16[2,128,1024]{1,2,0:T(8,128)(2,1)S(1)}, bf16[2,128,1024]{1,2,0:T(8,128)(2,1)S(1)}, u32[]{:S(2)}, u32[]{:S(2)}) collective-permute-start(bf16[2,128,1024]{1,2,0:T(8,128)(2,1)S(1)} %collective-permute-done), channel_id=1, source_target_pairs={{15,0},{0,1},{1,2},{2,3},{3,4},{4,5},{5,6},{6,7},{7,8},{8,9},{9,10... | collective-permute-start | bytes 1572872 | tf_op jit(solution)/shard_map/ppermute | solution.py:19
  20.2 11.5 %collective-permute-start.3 = (bf16[2,128,1024]{1,2,0:T(8,128)(2,1)S(1)}, bf16[2,128,1024]{1,2,0:T(8,128)(2,1)S(1)}, u32[]{:S(2)}, u32[]{:S(2)}) collective-permute-start(bf16[2,128,1024]{1,2,0:T(8,128)(2,1)S(1)} %collective-permute-done.2), channel_id=1, source_target_pairs={{1,0},{2,1},{3,2},{4,3},{5,4},{6,5},{7,6},{8,7},{9,8},{10,9},{11,1... | collective-permute-start | bytes 1572872 | tf_op jit(solution)/shard_map/ppermute | solution.py:19
  35.1 3.5 %copy-start = (bf16[8,128,640]{1,2,0:T(8,128)(2,1)}, bf16[8,128,640]{1,2,0:T(8,128)(2,1)S(1)}, u32[]{:S(2)}) copy-start(bf16[8,128,640]{1,2,0:T(8,128)(2,1)S(1)} %fusion) | copy-start | bytes 3932164
  47.8 4.8 %copy-start.4 = (f32[1,128,1024]{2,1,0:T(8,128)S(1)}, f32[1,128,1024]{2,1,0:T(8,128)}, u32[]{:S(2)}) copy-start(f32[1,128,1024]{2,1,0:T(8,128)} %copy.71) | copy-start | bytes 1572868
  47.8 4.8 %copy-start.5 = (f32[1,128,1024]{2,1,0:T(8,128)S(1)}, f32[1,128,1024]{2,1,0:T(8,128)}, u32[]{:S(2)}) copy-start(f32[1,128,1024]{2,1,0:T(8,128)} %copy.72) | copy-start | bytes 1572868
  50.2 25.7 %collective-permute-start.4 = (f32[2,128,1024]{2,1,0:T(8,128)}, f32[2,128,1024]{2,1,0:T(8,128)}, u32[]{:S(2)}, u32[]{:S(2)}) collective-permute-start(f32[2,128,1024]{2,1,0:T(8,128)} %pad_maximum_fusion), channel_id=1, source_target_pairs={{15,0},{0,1},{1,2},{2,3},{3,4},{4,5},{5,6},{6,7},{7,8},{8,9},{9,10... | collective-permute-start | bytes 3145736 | tf_op jit(solution)/shard_map/ppermute | solution.py:19
  53.8 27.4 %collective-permute-start.6 = (f32[2,128,1024]{2,1,0:T(8,128)}, f32[2,128,1024]{2,1,0:T(8,128)}, u32[]{:S(2)}, u32[]{:S(2)}) collective-permute-start(f32[2,128,1024]{2,1,0:T(8,128)} %pad_maximum_fusion.1), channel_id=1, source_target_pairs={{1,0},{2,1},{3,2},{4,3},{5,4},{6,5},{7,6},{8,7},{9,8},{10,9},{11,1... | collective-permute-start | bytes 3145736 | tf_op jit(solution)/shard_map/ppermute | solution.py:19
  68.2 12.9 %copy-start.2 = (f32[1,128,1024]{2,1,0:T(8,128)S(1)}, f32[1,128,1024]{2,1,0:T(8,128)}, u32[]{:S(2)}) copy-start(f32[1,128,1024]{2,1,0:T(8,128)} %copy.76) | copy-start | bytes 1572868
  68.3 12.9 %copy-start.3 = (f32[1,128,1024]{2,1,0:T(8,128)S(1)}, f32[1,128,1024]{2,1,0:T(8,128)}, u32[]{:S(2)}) copy-start(f32[1,128,1024]{2,1,0:T(8,128)} %copy.77) | copy-start | bytes 1572868
  78.6 4.8 %copy-start.1 = (bf16[8,128,640]{1,2,0:T(8,128)(2,1)S(1)}, bf16[8,128,640]{1,2,0:T(8,128)(2,1)}, u32[]{:S(2)}) copy-start(bf16[8,128,640]{1,2,0:T(8,128)(2,1)} %copy-done) | copy-start | bytes 3932164
  78.6 25.8 %collective-permute-start.5 = (f32[2,128,1024]{2,1,0:T(8,128)}, f32[2,128,1024]{2,1,0:T(8,128)}, u32[]{:S(2)}, u32[]{:S(2)}) collective-permute-start(f32[2,128,1024]{2,1,0:T(8,128)} %maximum_add_fusion.1), channel_id=1, source_target_pairs={{15,0},{0,1},{1,2},{2,3},{3,4},{4,5},{5,6},{6,7},{7,8},{8,9},{9,10... | collective-permute-start | bytes 3145736 | tf_op jit(solution)/shard_map/ppermute | solution.py:19
  83.5 21.0 %collective-permute-start.7 = (f32[2,128,1024]{2,1,0:T(8,128)}, f32[2,128,1024]{2,1,0:T(8,128)}, u32[]{:S(2)}, u32[]{:S(2)}) collective-permute-start(f32[2,128,1024]{2,1,0:T(8,128)} %maximum_add_fusion.2), channel_id=1, source_target_pairs={{1,0},{2,1},{3,2},{4,3},{5,4},{6,5},{7,6},{8,7},{9,8},{10,9},{11,1... | collective-permute-start | bytes 3145736 | tf_op jit(solution)/shard_map/ppermute | solution.py:19
where the time goes:
time: 109 us; the launch traced here: 108 us
  waiting for transfers between devices  44.2 us (41%)
  local copies, waits for them, and re-layouts  24.7 us (23%)
  matrix products  15.8 us (14%)
  other arithmetic  12 us (11%)
  starting transfers between devices  10.1 us (9%)
    ppermute x8, waiting for transfers between devices, from_behind(): return lax.ppermute(block, axis, route)  44.2 us
    another operation x10, local copies, waits for them, and re-layouts, pair_terms(): return jnp.stack((key_part, value_part)).reshape(2, tokens, row_width)  16.8 us
    ppermute x8, starting transfers between devices, from_behind(): return lax.ppermute(block, axis, route)  10.1 us
    dot_general x5, matrix products, pair_terms(): jnp.einsum('hqk,qhd->khd', grad_cols, query_heads, preferred_element_type...  7.73 us
    unnamed x24, local copies, waits for them, and re-layouts  5.46 us
    dot_general x5, matrix products, pair_terms(): jnp.einsum('hqk,qhd->khd', prob_cols, grad_heads, preferred_element_type=...  4.68 us
    another operation x2, other arithmetic, pair_terms(): return jnp.stack((key_part, value_part)).reshape(2, tokens, row_width)  3.47 us
    add x1, other arithmetic, body(): upward = upward + terms[SPAN - hop_index]  2.67 us
  transfers between devices with their start and end apart: 8, of which 5 were waited for; matrix products, arithmetic and copies ran while one was open for 26% of the time, Pallas kernels for 0%

commit v1 on v0

v1 whole, which is shorter than its diff:
```python
import functools
import math

import jax
import jax.numpy as jnp
from jax import lax
from jax.experimental import pallas as pl
from jax.experimental.pallas import tpu as pltpu
from jax.sharding import PartitionSpec as P

H = 8
SPAN = 2
NEG_FILL = -1e30

PARTNER, RELAY, SIBLING, PASSED, OWN = range(5)
BLOCKS = 2 * SPAN + 1


def kernel(
    devices,
    q_ref,
    k_ref,
    v_ref,
    do_ref,
    margin_ref,
    att_ref,
    gq_ref,
    gk_ref,
    gv_ref,
    kv,
    acc,
    bias,
    out_buf,
    in_buf,
    kv_send,
    kv_recv,
    pass_send,
    g_send,
    g_recv,
):
    tokens, width = q_ref.shape
    dim = width // H
    scale = 1.0 / math.sqrt(dim)
    me = lax.axis_index("view")
    core = lax.rem(me, 2)
    chip = me // 2
    odd = lax.rem(chip, 2)
    sign = 1 - 2 * odd
    sibling = me + 1 - 2 * core
    partner = me + 2 * sign
    onward = lax.rem(me + 4 * sign + devices, devices)
    source = lax.rem(me - 4 * sign + devices, devices)
    shared = lax.rem(odd + core, 2)

    def cols(h):
        return pl.ds(pl.multiple_of(h * dim, dim), dim)

    def rows(block):
        return pl.ds(block * tokens, tokens)

    def send(src, dst, send_sem, recv_sem, to):
        return pltpu.make_async_remote_copy(
            src_ref=src,
            dst_ref=dst,
            send_sem=send_sem,
            recv_sem=recv_sem,
            device_id={"view": to},
            device_id_type=pl.DeviceIdType.MESH,
        )

    def first(h, block, part, to):
        return send(
            (k_ref, v_ref)[part].at[:, cols(h)],
            kv.at[h, part, rows(block), :],
            kv_send.at[block, part, h],
            kv_recv.at[block, part, h],
            to,
        )

    def relay(h):
        return send(
            kv.at[h, :, rows(PARTNER), :],
            kv.at[h, :, rows(RELAY), :],
            pass_send.at[0, h],
            kv_recv.at[RELAY, 0, h],
            onward,
        )

    def forward(h, block):
        return send(
            kv.at[h, :, rows(block), :],
            kv.at[h, :, rows(PASSED), :],
            pass_send.at[1, h],
            kv_recv.at[PASSED, 0, h],
            sibling,
        )

    def grad(h, block, to):
        return send(
            out_buf.at[h, block],
            in_buf.at[h, block],
            g_send.at[block, h],
            g_recv.at[block, h],
            to,
        )

    barrier = pltpu.get_barrier_semaphore()
    for peer in (sibling, partner, onward, source):
        pl.semaphore_signal(
            barrier, inc=1, device_id={"view": peer}, device_id_type=pl.DeviceIdType.MESH
        )
    pl.semaphore_wait(barrier, 4)

    @pl.loop(0, H)
    def _(h):
        for part in range(2):
            first(h, PARTNER, part, partner).start()
        for part in range(2):
            first(h, SIBLING, part, sibling).start()

    side = 1 - 2 * core
    order = (2 * sign, -2 * sign, side, -side)
    for block, offset in enumerate(order):
        place = offset + SPAN - (offset + SPAN) // (SPAN + 1)
        mask = margin_ref[me, place].astype(jnp.float32)
        bias[:, block * tokens : (block + 1) * tokens] = jnp.full(
            (8, tokens), (1.0 - mask) * NEG_FILL, jnp.float32
        )
    bias[:, OWN * tokens :] = jnp.zeros((8, tokens), jnp.float32)
    for h in range(H):
        kv[h, 0, OWN * tokens :, :] = k_ref[:, h * dim : (h + 1) * dim]
        kv[h, 1, OWN * tokens :, :] = v_ref[:, h * dim : (h + 1) * dim]

    def dot(a, b, ca, cb):
        return lax.dot_general(a, b, (((ca,), (cb,)), ((), ())), preferred_element_type=jnp.float32)

    def compute(h):
        q = q_ref[:, cols(h)]
        do = do_ref[:, cols(h)]
        k_all = kv[h, 0]
        v_all = kv[h, 1]
        scores = dot(q, k_all, 1, 1) * scale + bias[0:1, :]
        e = jnp.exp(scores - jnp.max(scores, axis=-1, keepdims=True))
        prob = e * (1.0 / jnp.sum(e, axis=-1, keepdims=True))
        prob_half = prob.astype(jnp.bfloat16)
        att = dot(prob_half, v_all, 1, 0).astype(jnp.bfloat16)
        att_ref[:, cols(h)] = att
        row_dot = jnp.sum(
            do.astype(jnp.float32) * att.astype(jnp.float32), axis=-1, keepdims=True
        )
        prob_grad = dot(do, v_all, 1, 1)
        grad_half = (prob * (prob_grad - row_dot)).astype(jnp.bfloat16)
        gq_ref[:, cols(h)] = (dot(grad_half, k_all, 1, 0) * scale).astype(jnp.bfloat16)
        acc[h, 0] = dot(grad_half, q, 0, 0)
        acc[h, 1] = dot(prob_half, do, 0, 0)

    @pl.loop(0, H + 5)
    def _(t):
        @pl.when(t < H)
        def _():
            for part in range(2):
                first(t, PARTNER, part, partner).wait_recv()
            relay(t).start()

            @pl.when(shared == PARTNER)
            def _():
                forward(t, PARTNER).start()

        @pl.when((t >= 1) & (t < H + 1))
        def _():
            h = t - 1
            relay(h).wait_recv()

            @pl.when(shared == RELAY)
            def _():
                forward(h, RELAY).start()

        @pl.when((t >= 2) & (t < H + 2))
        def _():
            h = t - 2
            for part in range(2):
                first(h, SIBLING, part, sibling).wait_recv()
            forward(h, PARTNER).wait_recv()
            compute(h)
            for block in (PASSED, SIBLING):
                out_buf[h, block] = acc[h, :, block * tokens : (block + 1) * tokens, :].astype(
                    jnp.bfloat16
                )
                grad(h, block, sibling).start()

        @pl.when((t >= 3) & (t < H + 3))
        def _():
            h = t - 3
            grad(h, PASSED, sibling).wait_recv()
            place = pl.ds(pl.multiple_of(shared * tokens, tokens), tokens)
            acc[h, :, place, :] += in_buf[h, PASSED].astype(jnp.float32)
            out_buf[h, RELAY] = acc[h, :, RELAY * tokens : (RELAY + 1) * tokens, :].astype(
                jnp.bfloat16
            )
            grad(h, RELAY, source).start()

        @pl.when((t >= 4) & (t < H + 4))
        def _():
            h = t - 4
            grad(h, RELAY, source).wait_recv()
            out_buf[h, PARTNER] = (
                acc[h, :, :tokens, :] + in_buf[h, RELAY].astype(jnp.float32)
            ).astype(jnp.bfloat16)
            grad(h, PARTNER, partner).start()

        @pl.when(t >= 5)
        def _():
            h = t - 5
            grad(h, SIBLING, sibling).wait_recv()
            grad(h, PARTNER, partner).wait_recv()
            total = (
                acc[h, :, OWN * tokens :, :]
                + in_buf[h, SIBLING].astype(jnp.float32)
                + in_buf[h, PARTNER].astype(jnp.float32)
            )
            gk_ref[:, cols(h)] = (total[0] * scale).astype(jnp.bfloat16)
            gv_ref[:, cols(h)] = total[1].astype(jnp.bfloat16)

    @pl.loop(0, H)
    def _(h):
        for part in range(2):
            first(h, PARTNER, part, partner).wait_send()
            first(h, SIBLING, part, sibling).wait_send()
        relay(h).wait_send()
        forward(h, PARTNER).wait_send()
        grad(h, PASSED, sibling).wait_send()
        grad(h, SIBLING, sibling).wait_send()
        grad(h, RELAY, source).wait_send()
        grad(h, PARTNER, partner).wait_send()


def body(devices, query, keys, values, grad_out, margin):
    tokens, width = query.shape
    dim = width // H
    vmem = pl.BlockSpec(memory_space=pltpu.VMEM)
    shape = jax.ShapeDtypeStruct((tokens, width), jnp.bfloat16)
    dma = pltpu.SemaphoreType.DMA
    return pl.pallas_call(
        functools.partial(kernel, devices),
        out_shape=(shape,) * 4,
        in_specs=[vmem] * 4 + [pl.BlockSpec(memory_space=pltpu.SMEM)],
        out_specs=(vmem,) * 4,
        scratch_shapes=[
            pltpu.VMEM((H, 2, BLOCKS * tokens, dim), jnp.bfloat16),
            pltpu.VMEM((H, 2, BLOCKS * tokens, dim), jnp.float32),
            pltpu.VMEM((8, BLOCKS * tokens), jnp.float32),
            pltpu.VMEM((H, 4, 2, tokens, dim), jnp.bfloat16),
            pltpu.VMEM((H, 4, 2, tokens, dim), jnp.bfloat16),
            dma((4, 2, H)),
            dma((4, 2, H)),
            dma((2, H)),
            dma((4, H)),
            dma((4, H)),
        ],
        compiler_params=pltpu.CompilerParams(
            collective_id=0, has_side_effects=True, vmem_limit_bytes=40 * 1024 * 1024
        ),
    )(query, keys, values, grad_out, margin.reshape(margin.shape[:2]))


def solution(mesh):
    split = P(("groups", "view"), None)
    return jax.shard_map(
        functools.partial(body, mesh.shape["view"]),
        mesh=mesh,
        in_specs=(split,) * 4 + (P("groups", None, None, None),),
        out_specs=(split,) * 4,
        check_vma=False,
    )
```

time: 109 us -> 57.6 us (0.53)
  the two profiles are of different devices: /device:TPU:1 before, /device:TPU:0 now
where the time goes in v1:
time: 57.6 us; the launch traced here: 57.4 us
  Pallas kernels  49.3 us (86%)
  local copies, waits for them, and re-layouts  7.37 us (13%)
  between operations  0.64 us (1%)
    pallas_call x1, Pallas kernels, body(): pl.pallas_call(functools.partial(kernel, devices), out_shape=(shape,) * 4...  49.3 us
    unnamed x12, local copies, waits for them, and re-layouts  6.61 us

profile of v1, /device:TPU:0, one launch (start us, length us, event | category | flops | bytes accessed | tf_op | source)
XLA Modules:
  0.0 57.4 jit_solution(519218019360624851)
XLA Ops:
  0.6 0.8 %copy.9.margin_ref = s32[16,4]{1,0:T(8,128)S(1)} copy(s32[16,4]{0,1:T(4,128)} %bitcast.1) | data formatting | bytes 512 | tf_op jit(solution)/shard_map/reshape | solution.py:263
  1.4 0.0 copy-start
  1.4 0.9 %copy-done = bf16[128,1024]{1,0:T(8,128)(2,1)S(1)} copy-done((bf16[128,1024]{1,0:T(8,128)(2,1)S(1)}, bf16[128,1024]{1,0:T(8,128)(2,1)}, u32[]{:S(2)}) %copy-start) | copy-done | bytes 262168
  2.3 0.0 copy-start.1
  2.3 0.9 %copy-done.1 = bf16[128,1024]{1,0:T(8,128)(2,1)S(1)} copy-done((bf16[128,1024]{1,0:T(8,128)(2,1)S(1)}, bf16[128,1024]{1,0:T(8,128)(2,1)}, u32[]{:S(2)}) %copy-start.1) | copy-done | bytes 262168
  3.3 0.0 copy-start.2
  3.3 0.9 %copy-done.2 = bf16[128,1024]{1,0:T(8,128)(2,1)S(1)} copy-done((bf16[128,1024]{1,0:T(8,128)(2,1)S(1)}, bf16[128,1024]{1,0:T(8,128)(2,1)}, u32[]{:S(2)}) %copy-start.2) | copy-done | bytes 262168
  4.2 0.0 copy-start.3
  4.2 0.9 %copy-done.3 = bf16[128,1024]{1,0:T(8,128)(2,1)S(1)} copy-done((bf16[128,1024]{1,0:T(8,128)(2,1)S(1)}, bf16[128,1024]{1,0:T(8,128)(2,1)}, u32[]{:S(2)}) %copy-start.3) | copy-done | bytes 262168
  5.2 49.3 %shard_map.84 = (bf16[128,1024]{1,0:T(8,128)(2,1)S(1)}, bf16[128,1024]{1,0:T(8,128)(2,1)S(1)}, bf16[128,1024]{1,0:T(8,128)(2,1)S(1)}, bf16[128,1024]{1,0:T(8,128)(2,1)S(1)}) custom-call(bf16[128,1024]{1,0:T(8,128)(2,1)S(1)} %copy-done, bf16[128,1024]{1,0:T(8,128)(2,1)S(1)} %copy-done.1, bf16[128,1024]{1,0:T(8,128)(2,1)S(1)} %copy-done.2, ...), custom_call_target="tpu_custom_call" | custom-call | tf_op jit(solution)/shard_map/pallas_call | solution.py:243
  54.5 0.7 %copy.14 = bf16[128,1024]{1,0:T(8,128)(2,1)} copy(bf16[128,1024]{1,0:T(8,128)(2,1)S(1)} %get-tuple-element.8) | data formatting | bytes 524288
  55.2 0.7 %copy.15 = bf16[128,1024]{1,0:T(8,128)(2,1)} copy(bf16[128,1024]{1,0:T(8,128)(2,1)S(1)} %get-tuple-element.9) | data formatting | bytes 524288
  55.9 0.7 %copy.16 = bf16[128,1024]{1,0:T(8,128)(2,1)} copy(bf16[128,1024]{1,0:T(8,128)(2,1)S(1)} %get-tuple-element.10) | data formatting | bytes 524288
  56.6 0.7 %copy.17 = bf16[128,1024]{1,0:T(8,128)(2,1)} copy(bf16[128,1024]{1,0:T(8,128)(2,1)S(1)} %get-tuple-element.11) | data formatting | bytes 524288
Async XLA Ops:
  1.4 0.9 %copy-start = (bf16[128,1024]{1,0:T(8,128)(2,1)S(1)}, bf16[128,1024]{1,0:T(8,128)(2,1)}, u32[]{:S(2)}) copy-start(bf16[128,1024]{1,0:T(8,128)(2,1)} %q_ref.1) | copy-start | bytes 786436
  2.3 0.9 %copy-start.1 = (bf16[128,1024]{1,0:T(8,128)(2,1)S(1)}, bf16[128,1024]{1,0:T(8,128)(2,1)}, u32[]{:S(2)}) copy-start(bf16[128,1024]{1,0:T(8,128)(2,1)} %k_ref.1) | copy-start | bytes 786436
  3.3 0.9 %copy-start.2 = (bf16[128,1024]{1,0:T(8,128)(2,1)S(1)}, bf16[128,1024]{1,0:T(8,128)(2,1)}, u32[]{:S(2)}) copy-start(bf16[128,1024]{1,0:T(8,128)(2,1)} %v_ref.1) | copy-start | bytes 786436
  4.2 0.9 %copy-start.3 = (bf16[128,1024]{1,0:T(8,128)(2,1)S(1)}, bf16[128,1024]{1,0:T(8,128)(2,1)}, u32[]{:S(2)}) copy-start(bf16[128,1024]{1,0:T(8,128)(2,1)} %do_ref.1) | copy-start | bytes 786436

commit v2 on v1

--- a/solution.py
+++ b/solution.py
@@ -14,6 +14,10 @@
 
 PARTNER, RELAY, SIBLING, PASSED, OWN = range(5)
 BLOCKS = 2 * SPAN + 1
+
+AHEAD = 4
+
+RELAYED, READY, SUMMED, RETURNED, DONE = 3, 4, 5, 8, 11
 
 
 def kernel(
@@ -111,12 +115,14 @@
         )
     pl.semaphore_wait(barrier, 4)
 
-    @pl.loop(0, H)
-    def _(h):
+    def launch(h):
         for part in range(2):
             first(h, PARTNER, part, partner).start()
         for part in range(2):
             first(h, SIBLING, part, sibling).start()
+
+    for h in range(AHEAD):
+        launch(h)
 
     side = 1 - 2 * core
     order = (2 * sign, -2 * sign, side, -side)
@@ -154,7 +160,7 @@
         acc[h, 0] = dot(grad_half, q, 0, 0)
         acc[h, 1] = dot(prob_half, do, 0, 0)
 
-    @pl.loop(0, H + 5)
+    @pl.loop(0, H + DONE)
     def _(t):
         @pl.when(t < H)
         def _():
@@ -162,22 +168,26 @@
                 first(t, PARTNER, part, partner).wait_recv()
             relay(t).start()
 
+            @pl.when(t + AHEAD < H)
+            def _():
+                launch(t + AHEAD)
+
             @pl.when(shared == PARTNER)
             def _():
                 forward(t, PARTNER).start()
 
-        @pl.when((t >= 1) & (t < H + 1))
-        def _():
-            h = t - 1
+        @pl.when((t >= RELAYED) & (t < H + RELAYED))
+        def _():
+            h = t - RELAYED
             relay(h).wait_recv()
 
             @pl.when(shared == RELAY)
             def _():
                 forward(h, RELAY).start()
 
-        @pl.when((t >= 2) & (t < H + 2))
-        def _():
-            h = t - 2
+        @pl.when((t >= READY) & (t < H + READY))
+        def _():
+            h = t - READY
             for part in range(2):
                 first(h, SIBLING, part, sibling).wait_recv()
             forward(h, PARTNER).wait_recv()
@@ -188,9 +198,9 @@
                 )
                 grad(h, block, sibling).start()
 
-        @pl.when((t >= 3) & (t < H + 3))
-        def _():
-            h = t - 3
+        @pl.when((t >= SUMMED) & (t < H + SUMMED))
+        def _():
+            h = t - SUMMED
             grad(h, PASSED, sibling).wait_recv()
             place = pl.ds(pl.multiple_of(shared * tokens, tokens), tokens)
             acc[h, :, place, :] += in_buf[h, PASSED].astype(jnp.float32)
@@ -199,18 +209,18 @@
             )
             grad(h, RELAY, source).start()
 
-        @pl.when((t >= 4) & (t < H + 4))
-        def _():
-            h = t - 4
+        @pl.when((t >= RETURNED) & (t < H + RETURNED))
+        def _():
+            h = t - RETURNED
             grad(h, RELAY, source).wait_recv()
             out_buf[h, PARTNER] = (
                 acc[h, :, :tokens, :] + in_buf[h, RELAY].astype(jnp.float32)
             ).astype(jnp.bfloat16)
             grad(h, PARTNER, partner).start()
 
-        @pl.when(t >= 5)
-        def _():
-            h = t - 5
+        @pl.when(t >= DONE)
+        def _():
+            h = t - DONE
             grad(h, SIBLING, sibling).wait_recv()
             grad(h, PARTNER, partner).wait_recv()
             total = (

time: 57.6 us -> 49.3 us (0.86)
  Pallas kernels: 49.3 us -> 41 us
    pallas_call x1, Pallas kernels: 49.3 us -> 41 us  [body(): pl.pallas_call(functools.partial(kernel, devices), out_shape=(shape,) * 4...]
where the time goes in v2:
time: 49.3 us; the launch traced here: 49.1 us
  Pallas kernels  41 us (83%)
  local copies, waits for them, and re-layouts  7.37 us (15%)
  between operations  0.64 us (1%)
    pallas_call x1, Pallas kernels, body(): pl.pallas_call(functools.partial(kernel, devices), out_shape=(shape,) * 4...  41 us
    unnamed x12, local copies, waits for them, and re-layouts  6.61 us

profile of v2, /device:TPU:0, one launch (start us, length us, event | category | flops | bytes accessed | tf_op | source)
XLA Modules:
  0.0 49.1 jit_solution(4403717709741940354)
XLA Ops:
  0.6 0.8 %copy.9.margin_ref = s32[16,4]{1,0:T(8,128)S(1)} copy(s32[16,4]{0,1:T(4,128)} %bitcast.1) | data formatting | bytes 512 | tf_op jit(solution)/shard_map/reshape | solution.py:273
  1.4 0.0 copy-start
  1.4 0.9 %copy-done = bf16[128,1024]{1,0:T(8,128)(2,1)S(1)} copy-done((bf16[128,1024]{1,0:T(8,128)(2,1)S(1)}, bf16[128,1024]{1,0:T(8,128)(2,1)}, u32[]{:S(2)}) %copy-start) | copy-done | bytes 262168
  2.3 0.0 copy-start.1
  2.3 0.9 %copy-done.1 = bf16[128,1024]{1,0:T(8,128)(2,1)S(1)} copy-done((bf16[128,1024]{1,0:T(8,128)(2,1)S(1)}, bf16[128,1024]{1,0:T(8,128)(2,1)}, u32[]{:S(2)}) %copy-start.1) | copy-done | bytes 262168
  3.3 0.0 copy-start.2
  3.3 0.9 %copy-done.2 = bf16[128,1024]{1,0:T(8,128)(2,1)S(1)} copy-done((bf16[128,1024]{1,0:T(8,128)(2,1)S(1)}, bf16[128,1024]{1,0:T(8,128)(2,1)}, u32[]{:S(2)}) %copy-start.2) | copy-done | bytes 262168
  4.2 0.0 copy-start.3
  4.2 0.9 %copy-done.3 = bf16[128,1024]{1,0:T(8,128)(2,1)S(1)} copy-done((bf16[128,1024]{1,0:T(8,128)(2,1)S(1)}, bf16[128,1024]{1,0:T(8,128)(2,1)}, u32[]{:S(2)}) %copy-start.3) | copy-done | bytes 262168
  5.2 41.0 %shard_map.84 = (bf16[128,1024]{1,0:T(8,128)(2,1)S(1)}, bf16[128,1024]{1,0:T(8,128)(2,1)S(1)}, bf16[128,1024]{1,0:T(8,128)(2,1)S(1)}, bf16[128,1024]{1,0:T(8,128)(2,1)S(1)}) custom-call(bf16[128,1024]{1,0:T(8,128)(2,1)S(1)} %copy-done, bf16[128,1024]{1,0:T(8,128)(2,1)S(1)} %copy-done.1, bf16[128,1024]{1,0:T(8,128)(2,1)S(1)} %copy-done.2, ...), custom_call_target="tpu_custom_call" | custom-call | tf_op jit(solution)/shard_map/pallas_call | solution.py:253
  46.2 0.7 %copy.14 = bf16[128,1024]{1,0:T(8,128)(2,1)} copy(bf16[128,1024]{1,0:T(8,128)(2,1)S(1)} %get-tuple-element.8) | data formatting | bytes 524288
  47.0 0.7 %copy.15 = bf16[128,1024]{1,0:T(8,128)(2,1)} copy(bf16[128,1024]{1,0:T(8,128)(2,1)S(1)} %get-tuple-element.9) | data formatting | bytes 524288
  47.7 0.7 %copy.16 = bf16[128,1024]{1,0:T(8,128)(2,1)} copy(bf16[128,1024]{1,0:T(8,128)(2,1)S(1)} %get-tuple-element.10) | data formatting | bytes 524288
  48.4 0.7 %copy.17 = bf16[128,1024]{1,0:T(8,128)(2,1)} copy(bf16[128,1024]{1,0:T(8,128)(2,1)S(1)} %get-tuple-element.11) | data formatting | bytes 524288
Async XLA Ops:
  1.4 0.9 %copy-start = (bf16[128,1024]{1,0:T(8,128)(2,1)S(1)}, bf16[128,1024]{1,0:T(8,128)(2,1)}, u32[]{:S(2)}) copy-start(bf16[128,1024]{1,0:T(8,128)(2,1)} %q_ref.1) | copy-start | bytes 786436
  2.3 0.9 %copy-start.1 = (bf16[128,1024]{1,0:T(8,128)(2,1)S(1)}, bf16[128,1024]{1,0:T(8,128)(2,1)}, u32[]{:S(2)}) copy-start(bf16[128,1024]{1,0:T(8,128)(2,1)} %k_ref.1) | copy-start | bytes 786436
  3.3 0.9 %copy-start.2 = (bf16[128,1024]{1,0:T(8,128)(2,1)S(1)}, bf16[128,1024]{1,0:T(8,128)(2,1)}, u32[]{:S(2)}) copy-start(bf16[128,1024]{1,0:T(8,128)(2,1)} %v_ref.1) | copy-start | bytes 786436
  4.2 0.9 %copy-start.3 = (bf16[128,1024]{1,0:T(8,128)(2,1)S(1)}, bf16[128,1024]{1,0:T(8,128)(2,1)}, u32[]{:S(2)}) copy-start(bf16[128,1024]{1,0:T(8,128)(2,1)} %do_ref.1) | copy-start | bytes 786436

commit v3 on v2

--- a/solution.py
+++ b/solution.py
@@ -14,6 +14,7 @@
 
 PARTNER, RELAY, SIBLING, PASSED, OWN = range(5)
 BLOCKS = 2 * SPAN + 1
+VMEM_LIMIT = 60 * 1024 * 1024
 
 AHEAD = 4
 
@@ -22,11 +23,17 @@
 
 def kernel(
     devices,
+    q_hbm,
+    k_hbm,
+    v_hbm,
+    do_hbm,
+    margin_ref,
+    att_hbm,
+    gq_hbm,
+    gk_hbm,
+    gv_hbm,
     q_ref,
-    k_ref,
-    v_ref,
     do_ref,
-    margin_ref,
     att_ref,
     gq_ref,
     gk_ref,
@@ -36,13 +43,16 @@
     bias,
     out_buf,
     in_buf,
+    load_sem,
+    store_sem,
+    kv_load,
     kv_send,
     kv_recv,
     pass_send,
     g_send,
     g_recv,
 ):
-    tokens, width = q_ref.shape
+    tokens, width = q_hbm.shape
     dim = width // H
     scale = 1.0 / math.sqrt(dim)
     me = lax.axis_index("view")
@@ -72,12 +82,24 @@
             device_id_type=pl.DeviceIdType.MESH,
         )
 
-    def first(h, block, part, to):
+    def load(h, part):
+        return pltpu.make_async_copy(
+            (k_hbm, v_hbm)[part].at[:, cols(h)], kv.at[h, part, rows(OWN), :], kv_load.at[part, h]
+        )
+
+    def store(h, n):
+        return pltpu.make_async_copy(
+            (att_ref, gq_ref, gk_ref, gv_ref)[n].at[:, cols(h)],
+            (att_hbm, gq_hbm, gk_hbm, gv_hbm)[n].at[:, cols(h)],
+            store_sem.at[n, h],
+        )
+
+    def first(h, block, to):
         return send(
-            (k_ref, v_ref)[part].at[:, cols(h)],
-            kv.at[h, part, rows(block), :],
-            kv_send.at[block, part, h],
-            kv_recv.at[block, part, h],
+            kv.at[h, :, rows(OWN), :],
+            kv.at[h, :, rows(block), :],
+            kv_send.at[block, h],
+            kv_recv.at[block, h],
             to,
         )
 
@@ -86,7 +108,7 @@
             kv.at[h, :, rows(PARTNER), :],
             kv.at[h, :, rows(RELAY), :],
             pass_send.at[0, h],
-            kv_recv.at[RELAY, 0, h],
+            kv_recv.at[RELAY, h],
             onward,
         )
 
@@ -95,7 +117,7 @@
             kv.at[h, :, rows(block), :],
             kv.at[h, :, rows(PASSED), :],
             pass_send.at[1, h],
-            kv_recv.at[PASSED, 0, h],
+            kv_recv.at[PASSED, h],
             sibling,
         )
 
@@ -108,34 +130,41 @@
             to,
         )
 
+    loads = (
+        pltpu.make_async_copy(q_hbm, q_ref, load_sem.at[0]),
+        pltpu.make_async_copy(do_hbm, do_ref, load_sem.at[1]),
+    )
     barrier = pltpu.get_barrier_semaphore()
     for peer in (sibling, partner, onward, source):
         pl.semaphore_signal(
             barrier, inc=1, device_id={"view": peer}, device_id_type=pl.DeviceIdType.MESH
         )
-    pl.semaphore_wait(barrier, 4)
-
-    def launch(h):
+    for h in range(H):
         for part in range(2):
-            first(h, PARTNER, part, partner).start()
-        for part in range(2):
-            first(h, SIBLING, part, sibling).start()
-
-    for h in range(AHEAD):
-        launch(h)
-
+            load(h, part).start()
+    for copy in loads:
+        copy.start()
     side = 1 - 2 * core
     order = (2 * sign, -2 * sign, side, -side)
     for block, offset in enumerate(order):
         place = offset + SPAN - (offset + SPAN) // (SPAN + 1)
-        mask = margin_ref[me, place].astype(jnp.float32)
+        mask = margin_ref[place, me].astype(jnp.float32)
         bias[:, block * tokens : (block + 1) * tokens] = jnp.full(
             (8, tokens), (1.0 - mask) * NEG_FILL, jnp.float32
         )
     bias[:, OWN * tokens :] = jnp.zeros((8, tokens), jnp.float32)
-    for h in range(H):
-        kv[h, 0, OWN * tokens :, :] = k_ref[:, h * dim : (h + 1) * dim]
-        kv[h, 1, OWN * tokens :, :] = v_ref[:, h * dim : (h + 1) * dim]
+    pl.semaphore_wait(barrier, 4)
+
+    def launch(h):
+        for part in range(2):
+            load(h, part).wait()
+        first(h, PARTNER, partner).start()
+        first(h, SIBLING, sibling).start()
+
+    for h in range(AHEAD):
+        launch(h)
+    for copy in loads:
+        copy.wait()
 
     def dot(a, b, ca, cb):
         return lax.dot_general(a, b, (((ca,), (cb,)), ((), ())), preferred_element_type=jnp.float32)
@@ -164,8 +193,7 @@
     def _(t):
         @pl.when(t < H)
         def _():
-            for part in range(2):
-                first(t, PARTNER, part, partner).wait_recv()
+            first(t, PARTNER, partner).wait_recv()
             relay(t).start()
 
             @pl.when(t + AHEAD < H)
@@ -188,8 +216,7 @@
         @pl.when((t >= READY) & (t < H + READY))
         def _():
             h = t - READY
-            for part in range(2):
-                first(h, SIBLING, part, sibling).wait_recv()
+            first(h, SIBLING, sibling).wait_recv()
             forward(h, PARTNER).wait_recv()
             compute(h)
             for block in (PASSED, SIBLING):
@@ -197,6 +224,8 @@
                     jnp.bfloat16
                 )
                 grad(h, block, sibling).start()
+            store(h, 0).start()
+            store(h, 1).start()
 
         @pl.when((t >= SUMMED) & (t < H + SUMMED))
         def _():
@@ -230,47 +259,79 @@
             )
             gk_ref[:, cols(h)] = (total[0] * scale).astype(jnp.bfloat16)
             gv_ref[:, cols(h)] = total[1].astype(jnp.bfloat16)
+            store(h, 2).start()
+            store(h, 3).start()
 
     @pl.loop(0, H)
     def _(h):
-        for part in range(2):
-            first(h, PARTNER, part, partner).wait_send()
-            first(h, SIBLING, part, sibling).wait_send()
+        first(h, PARTNER, partner).wait_send()
+        first(h, SIBLING, sibling).wait_send()
         relay(h).wait_send()
         forward(h, PARTNER).wait_send()
         grad(h, PASSED, sibling).wait_send()
         grad(h, SIBLING, sibling).wait_send()
         grad(h, RELAY, source).wait_send()
         grad(h, PARTNER, partner).wait_send()
+        for n in range(4):
+            store(h, n).wait()
+
+
+def store_kernel(*refs):
+    sources, targets, held, sem = refs[:4], refs[4:8], refs[8], refs[9]
+    fetches = [
+        pltpu.make_async_copy(sources[n], held.at[n], sem.at[0, n]) for n in range(4)
+    ]
+    stores = [
+        pltpu.make_async_copy(held.at[n], targets[n], sem.at[1, n]) for n in range(4)
+    ]
+    for fetch in fetches:
+        fetch.start()
+    for fetch, store in zip(fetches, stores):
+        fetch.wait()
+        store.start()
+    for store in stores:
+        store.wait()
 
 
 def body(devices, query, keys, values, grad_out, margin):
     tokens, width = query.shape
     dim = width // H
-    vmem = pl.BlockSpec(memory_space=pltpu.VMEM)
+    hbm = pl.BlockSpec(memory_space=pltpu.HBM)
     shape = jax.ShapeDtypeStruct((tokens, width), jnp.bfloat16)
     dma = pltpu.SemaphoreType.DMA
-    return pl.pallas_call(
+    results = pl.pallas_call(
         functools.partial(kernel, devices),
         out_shape=(shape,) * 4,
-        in_specs=[vmem] * 4 + [pl.BlockSpec(memory_space=pltpu.SMEM)],
-        out_specs=(vmem,) * 4,
+        in_specs=[hbm] * 4 + [pl.BlockSpec(memory_space=pltpu.SMEM)],
+        out_specs=(hbm,) * 4,
         scratch_shapes=[
+            *[pltpu.VMEM((tokens, width), jnp.bfloat16)] * 6,
             pltpu.VMEM((H, 2, BLOCKS * tokens, dim), jnp.bfloat16),
             pltpu.VMEM((H, 2, BLOCKS * tokens, dim), jnp.float32),
             pltpu.VMEM((8, BLOCKS * tokens), jnp.float32),
             pltpu.VMEM((H, 4, 2, tokens, dim), jnp.bfloat16),
             pltpu.VMEM((H, 4, 2, tokens, dim), jnp.bfloat16),
-            dma((4, 2, H)),
-            dma((4, 2, H)),
+            dma((2,)),
+            dma((4, H)),
+            dma((2, H)),
+            dma((4, H)),
+            dma((4, H)),
             dma((2, H)),
             dma((4, H)),
             dma((4, H)),
         ],
         compiler_params=pltpu.CompilerParams(
-            collective_id=0, has_side_effects=True, vmem_limit_bytes=40 * 1024 * 1024
+            collective_id=0, has_side_effects=True, vmem_limit_bytes=VMEM_LIMIT
         ),
-    )(query, keys, values, grad_out, margin.reshape(margin.shape[:2]))
+    )(query, keys, values, grad_out, margin.reshape(margin.shape[:2]).T)
+    return pl.pallas_call(
+        store_kernel,
+        out_shape=(shape,) * 4,
+        in_specs=[hbm] * 4,
+        out_specs=(hbm,) * 4,
+        scratch_shapes=[pltpu.VMEM((4, tokens, width), jnp.bfloat16), dma((2, 4))],
+        compiler_params=pltpu.CompilerParams(vmem_limit_bytes=VMEM_LIMIT),
+    )(*results)
 
 
 def solution(mesh):

time: 49.3 us -> 44.2 us (0.90)
  local copies, waits for them, and re-layouts: 7.37 us -> 0 us
  Pallas kernels: 41 us -> 43.4 us
    unnamed x12 -> x0, local copies, waits for them, and re-layouts: 6.61 us -> none
    pallas_call x0 -> x1, Pallas kernels: none -> 1.98 us  [body(): pl.pallas_call(store_kernel, out_shape=(shape,) * 4, in_specs=[hbm] * 4,...]
    reshape x1 -> x0, local copies, waits for them, and re-layouts: 0.76 us -> none  [body(): margin.reshape(margin.shape[:2])]
where the time goes in v3:
time: 44.2 us; the launch traced here: 44.1 us
  Pallas kernels  43.4 us (98%)
  between operations  0.64 us (1%)
    pallas_call x1, Pallas kernels, body(): pl.pallas_call(functools.partial(kernel, devices), out_shape=(shape,) * 4...  41.4 us
    pallas_call x1, Pallas kernels, body(): pl.pallas_call(store_kernel, out_shape=(shape,) * 4, in_specs=[hbm] * 4,...  1.98 us

profile of v3, /device:TPU:0, one launch (start us, length us, event | category | flops | bytes accessed | tf_op | source)
XLA Modules:
  0.0 44.1 jit_solution(5665335458953304142)
XLA Ops:
  0.6 41.4 %shard_map.84 = (bf16[128,1024]{1,0:T(8,128)(2,1)}, bf16[128,1024]{1,0:T(8,128)(2,1)}, bf16[128,1024]{1,0:T(8,128)(2,1)}, bf16[128,1024]{1,0:T(8,128)(2,1)}) custom-call(bf16[128,1024]{1,0:T(8,128)(2,1)} %q_hbm.1, bf16[128,1024]{1,0:T(8,128)(2,1)} %k_hbm.1, bf16[128,1024]{1,0:T(8,128)(2,1)} %v_hbm.1, bf16[128,1024]{1,0:T(8,128)(2,1)} %do_hbm.1, s32[4,16]{1,0:T(4,128)} %bitcast.3), custom_call_target="tpu_custom_call" | custom-call | tf_op jit(solution)/shard_map/pallas_call | solution.py:302
  42.1 2.0 %shard_map.85 = (bf16[128,1024]{1,0:T(8,128)(2,1)}, bf16[128,1024]{1,0:T(8,128)(2,1)}, bf16[128,1024]{1,0:T(8,128)(2,1)}, bf16[128,1024]{1,0:T(8,128)(2,1)}) custom-call(bf16[128,1024]{1,0:T(8,128)(2,1)} %get-tuple-element.8.refs_0_, bf16[128,1024]{1,0:T(8,128)(2,1)} %get-tuple-element.9.refs_1_, bf16[128,1024]{1,0:T(8,128)(2,1)} %get-tuple-element.10.refs_2_, ...), custom_call_target="tpu_custom_call" | custom-call | tf_op jit(solution)/shard_map/pallas_call | solution.py:327

commit v4 on v3

--- a/solution.py
+++ b/solution.py
@@ -18,7 +18,7 @@
 
 AHEAD = 4
 
-RELAYED, READY, SUMMED, RETURNED, DONE = 3, 4, 5, 8, 11
+RELAYED, READY, SUMMED, RETURNED, DONE = 3, 5, 7, 11, 15
 
 
 def kernel(

time: 44.2 us -> 43.3 us (0.980)
  Pallas kernels: 43.4 us -> 42.5 us
    pallas_call x1, Pallas kernels: 41.4 us -> 40.5 us  [body(): pl.pallas_call(functools.partial(kernel, devices), out_shape=(shape,) * 4...]
where the time goes in v4:
time: 43.3 us; the launch traced here: 43.1 us
  Pallas kernels  42.5 us (98%)
  between operations  0.64 us (1%)
    pallas_call x1, Pallas kernels, body(): pl.pallas_call(functools.partial(kernel, devices), out_shape=(shape,) * 4...  40.5 us
    pallas_call x1, Pallas kernels, body(): pl.pallas_call(store_kernel, out_shape=(shape,) * 4, in_specs=[hbm] * 4,...  1.98 us

profile of v4, /device:TPU:0, one launch (start us, length us, event | category | flops | bytes accessed | tf_op | source)
XLA Modules:
  0.0 43.1 jit_solution(13175619920412074838)
XLA Ops:
  0.6 40.5 %shard_map.84 = (bf16[128,1024]{1,0:T(8,128)(2,1)}, bf16[128,1024]{1,0:T(8,128)(2,1)}, bf16[128,1024]{1,0:T(8,128)(2,1)}, bf16[128,1024]{1,0:T(8,128)(2,1)}) custom-call(bf16[128,1024]{1,0:T(8,128)(2,1)} %q_hbm.1, bf16[128,1024]{1,0:T(8,128)(2,1)} %k_hbm.1, bf16[128,1024]{1,0:T(8,128)(2,1)} %v_hbm.1, bf16[128,1024]{1,0:T(8,128)(2,1)} %do_hbm.1, s32[4,16]{1,0:T(4,128)} %bitcast.3), custom_call_target="tpu_custom_call" | custom-call | tf_op jit(solution)/shard_map/pallas_call | solution.py:302
  41.1 2.0 %shard_map.85 = (bf16[128,1024]{1,0:T(8,128)(2,1)}, bf16[128,1024]{1,0:T(8,128)(2,1)}, bf16[128,1024]{1,0:T(8,128)(2,1)}, bf16[128,1024]{1,0:T(8,128)(2,1)}) custom-call(bf16[128,1024]{1,0:T(8,128)(2,1)} %get-tuple-element.8.refs_0_, bf16[128,1024]{1,0:T(8,128)(2,1)} %get-tuple-element.9.refs_1_, bf16[128,1024]{1,0:T(8,128)(2,1)} %get-tuple-element.10.refs_2_, ...), custom_call_target="tpu_custom_call" | custom-call | tf_op jit(solution)/shard_map/pallas_call | solution.py:327

commit v5 on v4

--- a/solution.py
+++ b/solution.py
@@ -16,9 +16,9 @@
 BLOCKS = 2 * SPAN + 1
 VMEM_LIMIT = 60 * 1024 * 1024
 
-AHEAD = 4
-
-RELAYED, READY, SUMMED, RETURNED, DONE = 3, 5, 7, 11, 15
+AHEAD = 6
+
+RELAYED, READY, SUMMED, RETURNED, DONE = 4, 6, 8, 12, 16
 
 
 def kernel(

time: 43.3 us -> 43.2 us (level)
  no operation moved by 1% of the time
where the time goes in v5:
time: 43.2 us; the launch traced here: 43.1 us
  Pallas kernels  42.4 us (98%)
  between operations  0.64 us (1%)
    pallas_call x1, Pallas kernels, body(): pl.pallas_call(functools.partial(kernel, devices), out_shape=(shape,) * 4...  40.4 us
    pallas_call x1, Pallas kernels, body(): pl.pallas_call(store_kernel, out_shape=(shape,) * 4, in_specs=[hbm] * 4,...  1.98 us

profile of v5, /device:TPU:0, one launch (start us, length us, event | category | flops | bytes accessed | tf_op | source)
XLA Modules:
  0.0 43.1 jit_solution(17855212795580155516)
XLA Ops:
  0.6 40.4 %shard_map.84 = (bf16[128,1024]{1,0:T(8,128)(2,1)}, bf16[128,1024]{1,0:T(8,128)(2,1)}, bf16[128,1024]{1,0:T(8,128)(2,1)}, bf16[128,1024]{1,0:T(8,128)(2,1)}) custom-call(bf16[128,1024]{1,0:T(8,128)(2,1)} %q_hbm.1, bf16[128,1024]{1,0:T(8,128)(2,1)} %k_hbm.1, bf16[128,1024]{1,0:T(8,128)(2,1)} %v_hbm.1, bf16[128,1024]{1,0:T(8,128)(2,1)} %do_hbm.1, s32[4,16]{1,0:T(4,128)} %bitcast.3), custom_call_target="tpu_custom_call" | custom-call | tf_op jit(solution)/shard_map/pallas_call | solution.py:302
  41.1 2.0 %shard_map.85 = (bf16[128,1024]{1,0:T(8,128)(2,1)}, bf16[128,1024]{1,0:T(8,128)(2,1)}, bf16[128,1024]{1,0:T(8,128)(2,1)}, bf16[128,1024]{1,0:T(8,128)(2,1)}) custom-call(bf16[128,1024]{1,0:T(8,128)(2,1)} %get-tuple-element.8.refs_0_, bf16[128,1024]{1,0:T(8,128)(2,1)} %get-tuple-element.9.refs_1_, bf16[128,1024]{1,0:T(8,128)(2,1)} %get-tuple-element.10.refs_2_, ...), custom_call_target="tpu_custom_call" | custom-call | tf_op jit(solution)/shard_map/pallas_call | solution.py:327
